TPU v7x, 512 devices: a whole 4x8x8 slice. The times are simulated.
512 devices in a mesh: mem: 64 (over x, y, core), patch: 8 (over z).
Axes of the slice: x: 4, y: 8, z: 8, core: 2. Of those that a mesh axis runs over, the one named last changes fastest.
Arguments:
- state: bfloat16 [3, 1024, 131072], P(None, 'mem', 'patch'), may hold values from -6 to 6
- obs_noise: bfloat16 [1024, 131072], P('mem', 'patch'), may hold values from -6 to 6
- obs_values: float32 [8, 16384], P('patch', 'mem'), may hold values from -6 to 6
- obs_weights: bfloat16 [8, 128, 128, 128], P('patch', 'mem'), may hold values from -1 to 1
- tapers: float32 [8, 128, 128], replicated, may hold values from 0.2 to 1
- pair_source: int32 [8, 128, 4], P('patch', 'mem'), may hold values from 0 to 127, as said below
- pair_taper: int32 [8, 128, 4], P('patch', 'mem'), may hold values from 0 to 7
Outputs:
- analysis: bfloat16 [3, 1024, 131072], P(None, 'mem', 'patch')
Inputs may be any that keep to these rules, and one draw needn't show every extreme that they name: `pair_source`: each listed source lies in the same patch within 2 blocks of its target block; positions beyond the patch's ends are moved to its first or last block.
All inputs are finite; a program needn't handle non-finite values.
Results may differ from a plain program's by a relative error of at most 0.0058.
Values may be sent and summed in bfloat16 or wider, within the bound.
No kernel may reach another device: no remote copies, remote signals or barrier semaphores. Data moves between devices by JAX's collectives and lax.ppermute only.
A program may use at most 64 MiB of HBM per device.

v0:
```python
import jax
import jax.numpy as jnp
from jax import lax
from jax.sharding import PartitionSpec as P

MEMBERS = 1024
VARIABLES = 3
BLOCK_CELLS = 128
RADIUS = 2
PAIRS = 4
BLOCKS_DEV = 2


def padded(cells, sides, width):
    for axis, dim in sides:
        count = lax.axis_size(axis)
        ends = count - 1
        head = lax.slice_in_dim(cells, 0, width, axis=dim)
        tail = lax.slice_in_dim(cells, cells.shape[dim] - width, cells.shape[dim], axis=dim)
        cells = jnp.concatenate(
            [
                lax.ppermute(tail, axis, [(i, (i + 1) % count) for i in range(ends)]),
                cells,
                lax.ppermute(head, axis, [((i + 1) % count, i) for i in range(ends)]),
            ],
            axis=dim,
        )
    return cells


def centered(values):
    wide = values.astype(jnp.float32)
    return (wide - jnp.mean(wide, axis=-2, keepdims=True)).astype(jnp.bfloat16)


def on_device(state, obs_noise, obs_values, obs_weights, tapers, pair_source, pair_taper):
    columns = lax.all_to_all(state, "mem", split_axis=2, concat_axis=1, tiled=True)
    noise_cols = lax.all_to_all(obs_noise, "mem", split_axis=1, concat_axis=0, tiled=True)
    observed = columns[0]
    members = observed.shape[0]
    owned = observed.shape[1]
    anom_first = centered(observed)
    innovation = (
        obs_values[0][None, :] + noise_cols.astype(jnp.float32) - observed.astype(jnp.float32)
    ).astype(jnp.bfloat16)
    weighted = jnp.einsum(
        "nkd,kcd->nkc",
        innovation.reshape(members, BLOCKS_DEV, BLOCK_CELLS),
        obs_weights[0],
        preferred_element_type=jnp.float32,
    )
    weighted = weighted.astype(jnp.bfloat16).reshape(members, owned)
    window = padded(jnp.stack([anom_first, weighted]), (("mem", 2),), RADIUS * BLOCK_CELLS)
    anomalies = centered(columns)
    first_block = lax.axis_index("mem") * BLOCKS_DEV
    results = []
    for block in range(BLOCKS_DEV):
        target_anom = anomalies[:, :, block * BLOCK_CELLS : (block + 1) * BLOCK_CELLS]
        slices = []
        taper_tiles = []
        for slot in range(PAIRS):
            offset = (pair_source[0, block, slot] - first_block + RADIUS) * BLOCK_CELLS
            slices.append(lax.dynamic_slice_in_dim(window, offset, BLOCK_CELLS, 2))
            taper_tiles.append(
                lax.dynamic_index_in_dim(tapers, pair_taper[0, block, slot], 0, keepdims=False)
            )
        sources = jnp.concatenate(slices, axis=2)
        taper_row = jnp.concatenate(taper_tiles, axis=1)
        pieces = []
        for variable in range(VARIABLES):
            covariance = lax.dot_general(
                target_anom[variable],
                sources[0],
                (((0,), (0,)), ((), ())),
                preferred_element_type=jnp.float32,
            ) / (MEMBERS - 1)
            localized = (taper_row * covariance).astype(jnp.bfloat16)
            pieces.append(
                lax.dot_general(
                    sources[1],
                    localized,
                    (((1,), (1,)), ((), ())),
                    preferred_element_type=jnp.float32,
                )
            )
        total = jnp.stack(pieces)
        results.append(total)
    increment = jnp.concatenate(results, axis=2)
    updated = (columns.astype(jnp.float32) + increment).astype(jnp.bfloat16)
    return lax.all_to_all(updated, "mem", split_axis=1, concat_axis=2, tiled=True)


def solution(mesh):
    placed = (
        P(None, "mem", "patch"),
        P("mem", "patch"),
        P("patch", "mem"),
        P("patch", "mem", None, None),
        P(),
        P("patch", "mem", None),
        P("patch", "mem", None),
    )
    return jax.shard_map(
        on_device, mesh=mesh, in_specs=placed, out_specs=P(None, "mem", "patch"), check_vma=False
    )
```

profile of v0, /device:TPU:1, one launch (start us, length us, event | category | flops | bytes accessed | tf_op | source)
XLA Modules:
  0.0 259.1 jit_solution(17874046500938926867)
XLA Ops:
  0.0 0.0 copy-start
  0.0 2.0 copy.42
  2.0 11.6 %all-to-all-start.1 = ((bf16[16,64,256]{2,0,1:T(8,128)(2,1)}), bf16[16,64,256]{2,0,1:T(8,128)(2,1)S(1)}, u32[]{:S(2)}, u32[]{:S(2)}) async-start(bf16[16,64,256]{2,0,1:T(8,128)(2,1)} %bitcast.125), calls=%async_computation.1 | async-start | bytes 1048576 | tf_op jit(solution)/shard_map/all_to_all | solution.py:38
  13.7 15.7 %copy.24 = bf16[3,16,16384]{1,0,2:T(4,128)(2,1)} copy(bf16[3,16,16384]{2,1,0:T(8,128)(2,1)S(1)} %copy-done.9) | data formatting | bytes 3145728 | tf_op args[0]
  29.4 26.2 %reshape.70 = bf16[64,2,6144]{2,1,0:T(2,128)(2,1)} reshape(bf16[16384,3,16]{2,1,0:T(4,128)(2,1)} %bitcast.127) | data formatting | bytes 3145728
  55.6 0.0 all-to-all-done.1
  55.6 10.5 %all-to-all-start = ((bf16[64,2,6144]{2,1,0:T(2,128)(2,1)}), bf16[64,2,6144]{2,1,0:T(2,128)(2,1)S(1)}, u32[]{:S(2)}, u32[]{:S(2)}) async-start(bf16[64,2,6144]{2,1,0:T(2,128)(2,1)} %reshape.70), calls=%async_computation | async-start | bytes 3145728 | tf_op jit(solution)/shard_map/all_to_all | solution.py:37
  66.1 0.7 fusion.36
  71.9 0.7 fusion.35
  88.1 0.7 dynamic-slice_bitcast_fusion.7
  88.8 0.1 convert_bitcast_fusion
  88.9 1.5 reshape.68
  90.4 15.4 %all-to-all-done = bf16[64,2,6144]{2,1,0:T(2,128)(2,1)S(1)} async-done(((bf16[64,2,6144]{2,1,0:T(2,128)(2,1)}), bf16[64,2,6144]{2,1,0:T(2,128)(2,1)S(1)}, u32[]{:S(2)}, u32[]{:S(2)}) %all-to-all-start) | async-done | bytes 1572896 | tf_op jit(solution)/shard_map/all_to_all | solution.py:37
  105.9 21.0 %reshape.71 = bf16[16384,3,16]{2,1,0:T(4,128)(2,1)} reshape(bf16[64,2,6144]{2,1,0:T(2,128)(2,1)S(1)} %all-to-all-done) | data formatting | bytes 3145728
  126.9 15.3 %copy.36 = bf16[3,16,64,256]{3,2,1,0:T(8,128)(2,1)S(1)} copy(bf16[3,16,64,256]{1,0,3,2:T(4,128)(2,1)} %bitcast.126) | data formatting | bytes 3145728 | tf_op jit(solution)/shard_map/all_to_all | solution.py:37
  142.1 0.0 copy-start.2
  142.2 0.1 slice_convert_fusion
  142.3 0.2 fusion.15
  142.4 0.6 copy.27
  143.0 1.5 reshape.69
  144.6 2.1 subtract_convert_fusion.1
  146.7 1.1 convolution_convert_fusion
  147.8 1.2 copy.31
  149.0 0.1 fusion.13
  149.1 1.2 pad_maximum_fusion.3
  150.4 2.1 collective-permute-start.1
  152.5 3.7 %collective-permute-start = (bf16[2,1024,256]{2,1,0:T(8,128)(2,1)}, bf16[2,1024,256]{2,1,0:T(8,128)(2,1)}, u32[]{:S(2)}, u32[]{:S(2)}) collective-permute-start(bf16[2,1024,256]{2,1,0:T(8,128)(2,1)} %pad_maximum_fusion.3), channel_id=1, source_target_pairs={{0,8},{8,16},{16,24},{24,32},{32,40},{40,48},{48,56},{56,64},{64,7... | collective-permute-start | bytes 3145736 | tf_op jit(solution)/shard_map/ppermute | solution.py:22
  156.2 0.4 bitcast_convert_fusion
  156.6 1.8 copy.26
  158.4 2.3 copy.32
  160.7 1.7 convert_reduce_fusion
  162.5 1.4 subtract_convert_fusion
  163.9 2.9 %collective-permute-done.1 = bf16[2,1024,256]{2,1,0:T(8,128)(2,1)} collective-permute-done((bf16[2,1024,256]{2,1,0:T(8,128)(2,1)}, bf16[2,1024,256]{2,1,0:T(8,128)(2,1)}, u32[]{:S(2)}, u32[]{:S(2)}) %collective-permute-start.1) | collective-permute-done | bytes 1048608 | tf_op jit(solution)/shard_map/ppermute | solution.py:24
  166.8 1.2 collective-permute-done
  168.0 1.6 pad_maximum_fusion
  169.7 0.9 constant_dynamic-slice_fusion.7
  170.6 1.6 pad_maximum_fusion.1
  172.2 3.9 %convolution_bitcast_fusion = f32[1,1024,128]{1,2,0:T(8,128)} fusion(bf16[2,1024,512]{2,1,0:T(8,128)(2,1)} %get-tuple-element.38, bf16[3,1024,256]{2,1,0:T(8,128)(2,1)} %subtract_convert_fusion, f32[128,128]{1,0:T(8,128)S(1)} %copy-done.12, f32[128,128]{1,0:T(8,128)S(1)} %copy-done.13, f32[128,128]{1,0:T(8,128)S(1)} %get-tuple-element.14, ...), kind=kOutput, calls=%fused_computation.7 | convolution fusion | flops 268828672 | bytes 3145728 | tf_op jit(solution)/shard_map/dot_general | solution.py:79
  176.1 3.2 %convolution_bitcast_fusion.1 = f32[1,1024,128]{1,2,0:T(8,128)} fusion(bf16[2,1024,512]{2,1,0:T(8,128)(2,1)} %get-tuple-element.38, bf16[3,1024,256]{2,1,0:T(8,128)(2,1)} %subtract_convert_fusion, f32[128,128]{1,0:T(8,128)S(1)} %copy-done.12, f32[128,128]{1,0:T(8,128)S(1)} %copy-done.13, f32[128,128]{1,0:T(8,128)S(1)} %get-tuple-element.14, ...), kind=kOutput, calls=%fused_computation.8 | convolution fusion | flops 268828672 | bytes 3145728 | tf_op jit(solution)/shard_map/dot_general | solution.py:79
  179.3 3.2 %convolution_bitcast_fusion.2 = f32[1,1024,128]{1,2,0:T(8,128)} fusion(bf16[2,1024,512]{2,1,0:T(8,128)(2,1)} %get-tuple-element.38, bf16[3,1024,256]{2,1,0:T(8,128)(2,1)} %subtract_convert_fusion, f32[128,128]{1,0:T(8,128)S(1)} %copy-done.12, f32[128,128]{1,0:T(8,128)S(1)} %copy-done.13, f32[128,128]{1,0:T(8,128)S(1)} %get-tuple-element.14, ...), kind=kOutput, calls=%fused_computation.9 | convolution fusion | flops 268828672 | bytes 3145728 | tf_op jit(solution)/shard_map/dot_general | solution.py:79
  182.5 2.5 convolution_bitcast_fusion.3
  184.9 2.5 convolution_bitcast_fusion.4
  187.4 3.3 %convolution_bitcast_fusion.5 = f32[1,1024,128]{1,2,0:T(8,128)} fusion(bf16[2,1024,512]{2,1,0:T(8,128)(2,1)} %copy-done.8, bf16[3,1024,256]{2,1,0:T(8,128)(2,1)} %subtract_convert_fusion, f32[128,128]{1,0:T(8,128)S(1)} %get-tuple-element.16, f32[128,128]{1,0:T(8,128)S(1)} %get-tuple-element.17, f32[128,128]{1,0:T(8,128)S(1)} %get-tuple-element.18, ...), kind=kOutput, calls=%fused_computation.12 | convolution fusion | flops 268828672 | bytes 3145728 | tf_op jit(solution)/shard_map/dot_general | solution.py:79
  190.7 3.5 %fusion = bf16[3,1024,256]{1,2,0:T(8,128)(2,1)} fusion(f32[3,1024,256]{1,2,0:T(8,128)S(1)} %copy-done.3, f32[1,1024,128]{1,2,0:T(8,128)} %convolution_bitcast_fusion, f32[1,1024,128]{1,2,0:T(8,128)} %convolution_bitcast_fusion.1, f32[1,1024,128]{1,2,0:T(8,128)} %convolution_bitcast_fusion.2, f32[1,1024,128]{1,2,0:T(8,128)} %convolution_bitcast_fusion.3, ...), kind=kLoop, calls=%fused_computation.2 | loop fusion | flops 5505024 | bytes 7864320 | tf_op jit(solution)/shard_map/convert_element_type | solution.py:89
  194.2 2.9 %copy.33 = bf16[3,1024,256]{2,0,1:T(4,128)(2,1)S(1)} copy(bf16[3,1024,256]{1,2,0:T(8,128)(2,1)} %fusion) | data formatting | bytes 3145728 | tf_op jit(solution)/shard_map/convert_element_type | solution.py:89
  197.1 60.5 %all_to_all.46 = bf16[3,1024,256]{2,0,1:T(4,128)(2,1)S(1)} all-to-all(bf16[3,1024,256]{2,0,1:T(4,128)(2,1)S(1)} %copy.33), channel_id=1, replica_groups=mesh['mem'=64,'patch'=8] {'mem'}, dimensions={1} | all-to-all | bytes 3145728 | tf_op jit(solution)/shard_map/all_to_all | solution.py:90
  257.6 0.2 copy.34
  257.8 1.2 copy.38
  (34 shorter events, 0.1 us)
Async XLA Ops:
  0.0 146.6 %copy-start = (bf16[1,2,128,128]{3,2,1,0:T(8,128)(2,1)S(1)}, bf16[1,2,128,128]{3,2,1,0:T(8,128)(2,1)}, u32[]{:S(2)}) copy-start(bf16[1,2,128,128]{3,2,1,0:T(8,128)(2,1)} %param.10) | copy-start | bytes 196612
  0.0 13.6 %copy-start.9 = (bf16[3,16,16384]{2,1,0:T(8,128)(2,1)S(1)}, bf16[3,16,16384]{2,1,0:T(8,128)(2,1)}, u32[]{:S(2)}) copy-start(bf16[3,16,16384]{2,1,0:T(8,128)(2,1)} %param.7) | copy-start | bytes 4718596
  2.0 53.6 %all-to-all-start.1 = ((bf16[16,64,256]{2,0,1:T(8,128)(2,1)}), bf16[16,64,256]{2,0,1:T(8,128)(2,1)S(1)}, u32[]{:S(2)}, u32[]{:S(2)}) async-start(bf16[16,64,256]{2,0,1:T(8,128)(2,1)} %bitcast.125), calls=%async_computation.1 | async-start | bytes 1048576 | tf_op jit(solution)/shard_map/all_to_all | solution.py:38
  55.6 10.5 %copy-start.14 = (s32[1,2,4]{2,1,0:T(2,128)S(1)}, s32[1,2,4]{2,1,0:T(2,128)}, u32[]{:S(2)}) copy-start(s32[1,2,4]{2,1,0:T(2,128)} %param.12) | copy-start | bytes 100
  55.6 16.4 %copy-start.15 = (s32[1,2,4]{2,1,0:T(2,128)S(1)}, s32[1,2,4]{2,1,0:T(2,128)}, u32[]{:S(2)}) copy-start(s32[1,2,4]{2,1,0:T(2,128)} %param.13) | copy-start | bytes 100
  55.6 32.5 %copy-start.10 = (f32[8,128,128]{2,1,0:T(8,128)S(1)}, f32[8,128,128]{2,1,0:T(8,128)}, u32[]{:S(2)}) copy-start(f32[8,128,128]{2,1,0:T(8,128)} %param.11) | copy-start | bytes 1572868
  55.6 50.3 %all-to-all-start = ((bf16[64,2,6144]{2,1,0:T(2,128)(2,1)}), bf16[64,2,6144]{2,1,0:T(2,128)(2,1)S(1)}, u32[]{:S(2)}, u32[]{:S(2)}) async-start(bf16[64,2,6144]{2,1,0:T(2,128)(2,1)} %reshape.70), calls=%async_computation | async-start | bytes 3145728 | tf_op jit(solution)/shard_map/all_to_all | solution.py:37
  142.1 14.0 %copy-start.2 = (bf16[3,16,64,256]{3,2,1,0:T(8,128)(2,1)}, bf16[3,16,64,256]{3,2,1,0:T(8,128)(2,1)S(1)}, u32[]{:S(2)}) copy-start(bf16[3,16,64,256]{3,2,1,0:T(8,128)(2,1)S(1)} %copy.36) | copy-start | bytes 4718596
  142.4 2.1 copy-start.16
  149.0 7.1 %copy-start.4 = (bf16[1,1024,256]{2,1,0:T(8,128)(2,1)}, bf16[1,1024,256]{2,1,0:T(8,128)(2,1)S(1)}, u32[]{:S(2)}) copy-start(bf16[1,1024,256]{2,1,0:T(8,128)(2,1)S(1)} %copy.31) | copy-start | bytes 1572868
  149.1 3.3 %copy-start.6 = (bf16[1,1024,256]{2,1,0:T(8,128)(2,1)}, bf16[1,1024,256]{2,1,0:T(8,128)(2,1)S(1)}, u32[]{:S(2)}) copy-start(bf16[1,1024,256]{2,1,0:T(8,128)(2,1)S(1)} %fusion.13) | copy-start | bytes 1572868
  150.4 16.4 %collective-permute-start.1 = (bf16[2,1024,256]{2,1,0:T(8,128)(2,1)}, bf16[2,1024,256]{2,1,0:T(8,128)(2,1)}, u32[]{:S(2)}, u32[]{:S(2)}) collective-permute-start(bf16[2,1024,256]{2,1,0:T(8,128)(2,1)} %pad_maximum_fusion.3), channel_id=1, source_target_pairs={{8,0},{16,8},{24,16},{32,24},{40,32},{48,40},{56,48},{64,56},{72,6... | collective-permute-start | bytes 3145736 | tf_op jit(solution)/shard_map/ppermute | solution.py:24
  152.5 15.5 %collective-permute-start = (bf16[2,1024,256]{2,1,0:T(8,128)(2,1)}, bf16[2,1024,256]{2,1,0:T(8,128)(2,1)}, u32[]{:S(2)}, u32[]{:S(2)}) collective-permute-start(bf16[2,1024,256]{2,1,0:T(8,128)(2,1)} %pad_maximum_fusion.3), channel_id=1, source_target_pairs={{0,8},{8,16},{16,24},{24,32},{32,40},{40,48},{48,56},{56,64},{64,7... | collective-permute-start | bytes 3145736 | tf_op jit(solution)/shard_map/ppermute | solution.py:22
  162.4 5.6 %copy-start.5 = (bf16[1,1024,256]{2,1,0:T(8,128)(2,1)S(1)}, bf16[1,1024,256]{2,1,0:T(8,128)(2,1)}, u32[]{:S(2)}) copy-start(bf16[1,1024,256]{2,1,0:T(8,128)(2,1)} %copy-done.4) | copy-start | bytes 1572868
  162.5 5.6 %copy-start.7 = (bf16[1,1024,256]{2,1,0:T(8,128)(2,1)S(1)}, bf16[1,1024,256]{2,1,0:T(8,128)(2,1)}, u32[]{:S(2)}) copy-start(bf16[1,1024,256]{2,1,0:T(8,128)(2,1)} %copy-done.6) | copy-start | bytes 1572868
  170.5 1.6 copy-start.11
  170.6 1.6 copy-start.12
  170.6 1.6 copy-start.13
  172.2 12.8 %copy-start.8 = (bf16[2,1024,512]{2,1,0:T(8,128)(2,1)}, bf16[2,1024,512]{2,1,0:T(8,128)(2,1)S(1)}, u32[]{:S(2)}) copy-start(bf16[2,1024,512]{2,1,0:T(8,128)(2,1)S(1)} %get-tuple-element.37) | copy-start | bytes 6291460
  187.4 3.3 %copy-start.3 = (f32[3,1024,256]{1,2,0:T(8,128)S(1)}, f32[3,1024,256]{1,2,0:T(8,128)}, u32[]{:S(2)}) copy-start(f32[3,1024,256]{1,2,0:T(8,128)} %copy.32) | copy-start | bytes 9437188
  257.6 1.5 copy-start.1
where the time goes:
time: 261 us; the launch traced here: 259 us
  local copies, waits for them, and re-layouts  96.7 us (37%)
  blocking collectives  60.5 us (23%)
  starting transfers between devices  27.8 us (11%)
  between operations  20.9 us (8%)
  matrix products  19.6 us (8%)
  waiting for transfers between devices  19.5 us (7%)
  other arithmetic  14 us (5%)
    unnamed x37, local copies, waits for them, and re-layouts  63 us
    all_to_all x1, blocking collectives, on_device(): lax.all_to_all(updated, 'mem', split_axis=1, concat_axis=2, tiled=True)  60.5 us
    dot_general x6, matrix products, on_device(): lax.dot_general(sources[1], localized, (((1,), (1,)), ((), ())), preferre...  18.5 us
    all_to_all x1, waiting for transfers between devices, on_device(): lax.all_to_all(state, 'mem', split_axis=2, concat_axis=1, tiled=True)  15.4 us
    all_to_all x1, local copies, waits for them, and re-layouts, on_device(): lax.all_to_all(state, 'mem', split_axis=2, concat_axis=1, tiled=True)  15.3 us
    all_to_all x1, starting transfers between devices, on_device(): lax.all_to_all(obs_noise, 'mem', split_axis=1, concat_axis=0, tiled=True)  11.6 us
    all_to_all x1, starting transfers between devices, on_device(): lax.all_to_all(state, 'mem', split_axis=2, concat_axis=1, tiled=True)  10.5 us
    convert_element_type x3, local copies, waits for them, and re-layouts, on_device(): updated = (columns.astype(jnp.float32) + increment).astype(jnp.bfloat16)  7.09 us
  transfers between devices with their start and end apart: 4, of which 3 were waited for; matrix products, arithmetic and copies ran while one was open for 21% of the time, Pallas kernels for 0%

commit v1 on v0

--- a/solution.py
+++ b/solution.py
@@ -34,7 +34,10 @@
 
 
 def on_device(state, obs_noise, obs_values, obs_weights, tapers, pair_source, pair_taper):
-    columns = lax.all_to_all(state, "mem", split_axis=2, concat_axis=1, tiled=True)
+    columns = jnp.concatenate(
+        lax.all_to_all(jnp.stack(jnp.split(state, lax.axis_size("mem"), axis=2)), "mem", 0, 0),
+        axis=1,
+    )
     noise_cols = lax.all_to_all(obs_noise, "mem", split_axis=1, concat_axis=0, tiled=True)
     observed = columns[0]
     members = observed.shape[0]

time: 261 us -> 241 us (0.923)
  local copies, waits for them, and re-layouts: 96.7 us -> 59.3 us
  waiting for transfers between devices: 19.5 us -> 38.1 us
  other arithmetic: 14 us -> 17.6 us
  blocking collectives: 60.5 us -> 57.1 us
    unnamed x37 -> x93, local copies, waits for them, and re-layouts: 63 us -> 39.5 us
    all_to_all x1, waiting for transfers between devices: 15.4 us -> 38.1 us  [on_device(): lax.all_to_all(jnp.stack(jnp.split(state, lax.axis_size('mem'), axis=2)),...]
    all_to_all x1 -> x0, local copies, waits for them, and re-layouts: 15.3 us -> none  [on_device(): lax.all_to_all(state, 'mem', split_axis=2, concat_axis=1, tiled=True)]
    all_to_all x1, blocking collectives: 60.5 us -> 57.1 us  [on_device(): lax.all_to_all(updated, 'mem', split_axis=1, concat_axis=2, tiled=True)]
    convert_element_type x2, local copies, waits for them, and re-layouts: 2.13 us -> 5.28 us  [centered(): wide = values.astype(jnp.float32)]
    ppermute x1, waiting for transfers between devices: 2.92 us -> 0.01 us  [padded(): lax.ppermute(head, axis, [((i + 1) % count, i) for i in range(ends)])]
    convert_element_type x3 -> x2, local copies, waits for them, and re-layouts: 7.09 us -> 5.26 us  [on_device(): updated = (columns.astype(jnp.float32) + increment).astype(jnp.bfloat16)]
  transfers between devices with their start and end apart: 4 -> 4, of which waited for: 3 -> 1; matrix products, arithmetic and copies ran while one was open for 21% -> 21% of each run, Pallas kernels for 0% -> 0%
where the time goes in v1:
time: 241 us; the launch traced here: 240 us
  local copies, waits for them, and re-layouts  59.3 us (25%)
  blocking collectives  57.1 us (24%)
  waiting for transfers between devices  38.1 us (16%)
  starting transfers between devices  27.8 us (12%)
  between operations  20.7 us (9%)
  matrix products  18.9 us (8%)
  other arithmetic  17.6 us (7%)
    all_to_all x1, blocking collectives, on_device(): lax.all_to_all(updated, 'mem', split_axis=1, concat_axis=2, tiled=True)  57.1 us
    unnamed x93, local copies, waits for them, and re-layouts  39.5 us
    all_to_all x1, waiting for transfers between devices, on_device(): lax.all_to_all(jnp.stack(jnp.split(state, lax.axis_size('mem'), axis=2)),...  38.1 us
    dot_general x6, matrix products, on_device(): lax.dot_general(sources[1], localized, (((1,), (1,)), ((), ())), preferre...  18.6 us
    all_to_all x1, starting transfers between devices, on_device(): lax.all_to_all(obs_noise, 'mem', split_axis=1, concat_axis=0, tiled=True)  11.6 us
    all_to_all x1, starting transfers between devices, on_device(): lax.all_to_all(jnp.stack(jnp.split(state, lax.axis_size('mem'), axis=2)),...  10.5 us
    convert_element_type x2, local copies, waits for them, and re-layouts, centered(): wide = values.astype(jnp.float32)  5.28 us
    convert_element_type x2, local copies, waits for them, and re-layouts, on_device(): updated = (columns.astype(jnp.float32) + increment).astype(jnp.bfloat16)  5.26 us
  transfers between devices with their start and end apart: 4, of which 1 were waited for; matrix products, arithmetic and copies ran while one was open for 21% of the time, Pallas kernels for 0%

profile of v1, /device:TPU:1, one launch (start us, length us, event | category | flops | bytes accessed | tf_op | source)
XLA Modules:
  0.0 239.5 jit_solution(1340998057227788498)
XLA Ops:
  0.0 2.0 copy.41
  2.0 11.6 %all-to-all-start.1 = ((bf16[16,64,256]{2,0,1:T(8,128)(2,1)}), bf16[16,64,256]{2,0,1:T(8,128)(2,1)S(1)}, u32[]{:S(2)}, u32[]{:S(2)}) async-start(bf16[16,64,256]{2,0,1:T(8,128)(2,1)} %bitcast.250), calls=%async_computation.1 | async-start | bytes 1048576 | tf_op jit(solution)/shard_map/all_to_all | solution.py:41
  13.7 0.6 constant_dynamic-update-slice_fusion.63
  16.1 0.6 constant_dynamic-update-slice_fusion.59
  16.7 0.6 constant_dynamic-update-slice_fusion.58
  17.3 0.6 constant_dynamic-update-slice_fusion.57
  17.9 0.6 constant_dynamic-update-slice_fusion.56
  18.5 0.6 constant_dynamic-update-slice_fusion.55
  19.2 0.6 constant_dynamic-update-slice_fusion.54
  19.8 0.6 constant_dynamic-update-slice_fusion.53
  20.4 0.6 constant_dynamic-update-slice_fusion.52
  21.0 0.6 constant_dynamic-update-slice_fusion.51
  21.6 0.6 constant_dynamic-update-slice_fusion.50
  22.2 0.6 constant_dynamic-update-slice_fusion.49
  22.8 0.6 constant_dynamic-update-slice_fusion.48
  27.7 0.6 constant_dynamic-update-slice_fusion.40
  52.8 10.5 %all-to-all-start = ((bf16[64,3,16,256]{3,2,1,0:T(8,128)(2,1)}), bf16[64,3,16,256]{3,2,1,0:T(8,128)(2,1)}, u32[]{:S(2)}, u32[]{:S(2)}) async-start(bf16[64,3,16,256]{3,2,1,0:T(8,128)(2,1)} %constant_dynamic-update-slice_fusion), calls=%async_computation | async-start | bytes 3145728 | tf_op jit(solution)/shard_map/all_to_all | solution.py:38
  63.4 1.5 reshape.73
  64.9 38.1 %all-to-all-done = bf16[64,3,16,256]{3,2,1,0:T(8,128)(2,1)} async-done(((bf16[64,3,16,256]{3,2,1,0:T(8,128)(2,1)}), bf16[64,3,16,256]{3,2,1,0:T(8,128)(2,1)}, u32[]{:S(2)}, u32[]{:S(2)}) %all-to-all-start) | async-done | bytes 1572896 | tf_op jit(solution)/shard_map/all_to_all | solution.py:38
  103.0 1.9 copy_bitcast_fusion
  105.1 1.1 slice_convert_fusion
  106.2 2.7 %reshape.74 = f32[1024,2,128]{2,1,0:T(2,128)} reshape(f32[1,64,16,256]{3,2,1,0:T(8,128)} %slice_convert_fusion) | data formatting | bytes 2097152 | tf_op jit(solution)/shard_map/convert_element_type | solution.py:32
  108.9 2.5 %copy.24 = f32[1,1024,256]{1,2,0:T(8,128)} copy(f32[1,1024,256]{2,1,0:T(8,128)} %bitcast.252) | data formatting | bytes 2097152 | tf_op jit(solution)/shard_map/convert_element_type | solution.py:32
  111.5 1.4 subtract_convert_fusion.2
  113.0 1.9 subtract_convert_fusion.1
  115.3 0.8 copy-done.2
  116.1 1.1 pad_maximum_fusion.3
  117.2 2.1 collective-permute-start.1
  119.2 3.7 %collective-permute-start = (bf16[2,1024,256]{1,2,0:T(8,128)(2,1)}, bf16[2,1024,256]{1,2,0:T(8,128)(2,1)}, u32[]{:S(2)}, u32[]{:S(2)}) collective-permute-start(bf16[2,1024,256]{1,2,0:T(8,128)(2,1)} %pad_maximum_fusion.3), channel_id=1, source_target_pairs={{0,8},{8,16},{16,24},{24,32},{32,40},{40,48},{48,56},{56,64},{64,7... | collective-permute-start | bytes 3145736 | tf_op jit(solution)/shard_map/ppermute | solution.py:22
  122.9 0.7 fusion.36
  128.7 0.7 fusion.35
  144.7 1.8 dynamic-slice_bitcast_fusion.7
  146.5 2.3 copy.27
  148.8 1.7 convert_reduce_fusion
  150.5 1.4 subtract_convert_fusion
  151.9 1.8 pad_maximum_fusion
  153.7 0.6 constant_dynamic-slice_fusion.7
  154.4 1.6 pad_maximum_fusion.1
  155.9 3.9 %convolution_bitcast_fusion = f32[1,1024,128]{1,2,0:T(8,128)} fusion(bf16[2,1024,512]{1,2,0:T(8,128)(2,1)} %get-tuple-element.40, bf16[3,1024,256]{2,1,0:T(8,128)(2,1)} %subtract_convert_fusion, f32[128,128]{1,0:T(8,128)S(1)} %copy-done.10, f32[128,128]{1,0:T(8,128)S(1)} %copy-done.11, f32[128,128]{1,0:T(8,128)S(1)} %get-tuple-element.16, ...), kind=kOutput, calls=%fused_computation.8 | convolution fusion | flops 268828672 | bytes 3145728 | tf_op jit(solution)/shard_map/dot_general | solution.py:82
  159.9 3.2 %convolution_bitcast_fusion.1 = f32[1,1024,128]{1,2,0:T(8,128)} fusion(bf16[2,1024,512]{1,2,0:T(8,128)(2,1)} %get-tuple-element.40, bf16[3,1024,256]{2,1,0:T(8,128)(2,1)} %subtract_convert_fusion, f32[128,128]{1,0:T(8,128)S(1)} %copy-done.10, f32[128,128]{1,0:T(8,128)S(1)} %copy-done.11, f32[128,128]{1,0:T(8,128)S(1)} %get-tuple-element.16, ...), kind=kOutput, calls=%fused_computation.9 | convolution fusion | flops 268828672 | bytes 3145728 | tf_op jit(solution)/shard_map/dot_general | solution.py:82
  163.1 3.2 %convolution_bitcast_fusion.2 = f32[1,1024,128]{1,2,0:T(8,128)} fusion(bf16[2,1024,512]{1,2,0:T(8,128)(2,1)} %get-tuple-element.40, bf16[3,1024,256]{2,1,0:T(8,128)(2,1)} %subtract_convert_fusion, f32[128,128]{1,0:T(8,128)S(1)} %copy-done.10, f32[128,128]{1,0:T(8,128)S(1)} %copy-done.11, f32[128,128]{1,0:T(8,128)S(1)} %get-tuple-element.16, ...), kind=kOutput, calls=%fused_computation.10 | convolution fusion | flops 268828672 | bytes 3145728 | tf_op jit(solution)/shard_map/dot_general | solution.py:82
  166.3 2.5 %convolution_bitcast_fusion.3 = f32[1,1024,128]{1,2,0:T(8,128)} fusion(bf16[2,1024,512]{1,2,0:T(8,128)(2,1)S(1)} %get-tuple-element.39, bf16[3,1024,256]{2,1,0:T(8,128)(2,1)} %subtract_convert_fusion, f32[128,128]{1,0:T(8,128)S(1)} %get-tuple-element.18, f32[128,128]{1,0:T(8,128)S(1)} %get-tuple-element.19, f32[128,128]{1,0:T(8,128)S(1)} %get-tuple-element.20, ...), kind=kOutput, calls=%fused_computation.11 | convolution fusion | flops 268828672 | bytes 3145728 | tf_op jit(solution)/shard_map/dot_general | solution.py:82
  168.8 2.5 %convolution_bitcast_fusion.4 = f32[1,1024,128]{1,2,0:T(8,128)} fusion(bf16[2,1024,512]{1,2,0:T(8,128)(2,1)S(1)} %get-tuple-element.39, bf16[3,1024,256]{2,1,0:T(8,128)(2,1)} %subtract_convert_fusion, f32[128,128]{1,0:T(8,128)S(1)} %get-tuple-element.18, f32[128,128]{1,0:T(8,128)S(1)} %get-tuple-element.19, f32[128,128]{1,0:T(8,128)S(1)} %get-tuple-element.20, ...), kind=kOutput, calls=%fused_computation.12 | convolution fusion | flops 268828672 | bytes 3145728 | tf_op jit(solution)/shard_map/dot_general | solution.py:82
  171.3 3.3 %convolution_bitcast_fusion.5 = f32[1,1024,128]{1,2,0:T(8,128)} fusion(bf16[2,1024,512]{1,2,0:T(8,128)(2,1)} %copy-done.7, bf16[3,1024,256]{2,1,0:T(8,128)(2,1)} %subtract_convert_fusion, f32[128,128]{1,0:T(8,128)S(1)} %get-tuple-element.18, f32[128,128]{1,0:T(8,128)S(1)} %get-tuple-element.19, f32[128,128]{1,0:T(8,128)S(1)} %get-tuple-element.20, ...), kind=kOutput, calls=%fused_computation.13 | convolution fusion | flops 268828672 | bytes 3145728 | tf_op jit(solution)/shard_map/dot_general | solution.py:82
  174.6 3.5 %fusion = bf16[3,1024,256]{1,2,0:T(8,128)(2,1)} fusion(f32[3,1024,256]{1,2,0:T(8,128)S(1)} %copy-done.1, f32[1,1024,128]{1,2,0:T(8,128)} %convolution_bitcast_fusion, f32[1,1024,128]{1,2,0:T(8,128)} %convolution_bitcast_fusion.1, f32[1,1024,128]{1,2,0:T(8,128)} %convolution_bitcast_fusion.2, f32[1,1024,128]{1,2,0:T(8,128)} %convolution_bitcast_fusion.3, ...), kind=kLoop, calls=%fused_computation.2 | loop fusion | flops 5505024 | bytes 7864320 | tf_op jit(solution)/shard_map/convert_element_type | solution.py:92
  178.0 2.9 %copy.28 = bf16[3,1024,256]{2,0,1:T(4,128)(2,1)S(1)} copy(bf16[3,1024,256]{1,2,0:T(8,128)(2,1)} %fusion) | data formatting | bytes 3145728 | tf_op jit(solution)/shard_map/convert_element_type | solution.py:92
  181.0 57.1 %all_to_all.36 = bf16[3,1024,256]{2,0,1:T(4,128)(2,1)S(1)} all-to-all(bf16[3,1024,256]{2,0,1:T(4,128)(2,1)S(1)} %copy.28), channel_id=1, replica_groups=mesh['mem'=64,'patch'=8] {'mem'}, dimensions={1} | all-to-all | bytes 3145728 | tf_op jit(solution)/shard_map/all_to_all | solution.py:93
  238.3 1.2 copy.32
  (88 shorter events, 31.5 us)
Async XLA Ops:
  0.0 114.9 %copy-start = (bf16[1,2,128,128]{3,2,1,0:T(8,128)(2,1)S(1)}, bf16[1,2,128,128]{3,2,1,0:T(8,128)(2,1)}, u32[]{:S(2)}) copy-start(bf16[1,2,128,128]{3,2,1,0:T(8,128)(2,1)} %param.10) | copy-start | bytes 196612
  0.0 13.6 %copy-start.8 = (bf16[3,16,16384]{2,1,0:T(8,128)(2,1)S(1)}, bf16[3,16,16384]{2,1,0:T(8,128)(2,1)}, u32[]{:S(2)}) copy-start(bf16[3,16,16384]{2,1,0:T(8,128)(2,1)} %param.7) | copy-start | bytes 4718596
  2.0 50.8 %all-to-all-start.1 = ((bf16[16,64,256]{2,0,1:T(8,128)(2,1)}), bf16[16,64,256]{2,0,1:T(8,128)(2,1)S(1)}, u32[]{:S(2)}, u32[]{:S(2)}) async-start(bf16[16,64,256]{2,0,1:T(8,128)(2,1)} %bitcast.250), calls=%async_computation.1 | async-start | bytes 1048576 | tf_op jit(solution)/shard_map/all_to_all | solution.py:41
  52.8 50.2 %all-to-all-start = ((bf16[64,3,16,256]{3,2,1,0:T(8,128)(2,1)}), bf16[64,3,16,256]{3,2,1,0:T(8,128)(2,1)}, u32[]{:S(2)}, u32[]{:S(2)}) async-start(bf16[64,3,16,256]{3,2,1,0:T(8,128)(2,1)} %constant_dynamic-update-slice_fusion), calls=%async_computation | async-start | bytes 3145728 | tf_op jit(solution)/shard_map/all_to_all | solution.py:38
  108.9 4.0 %copy-start.14 = (f32[1,256]{1,0:T(1,128)S(1)}, f32[1,256]{1,0:T(1,128)}, u32[]{:S(2)}) copy-start(f32[1,256]{1,0:T(1,128)} %param.9) | copy-start | bytes 3076
  111.5 1.5 copy-start.6
  112.9 2.3 copy-start.4
  114.9 8.0 %copy-start.12 = (s32[1,2,4]{2,1,0:T(2,128)S(1)}, s32[1,2,4]{2,1,0:T(2,128)}, u32[]{:S(2)}) copy-start(s32[1,2,4]{2,1,0:T(2,128)} %param.12) | copy-start | bytes 100
  114.9 13.8 %copy-start.13 = (s32[1,2,4]{2,1,0:T(2,128)S(1)}, s32[1,2,4]{2,1,0:T(2,128)}, u32[]{:S(2)}) copy-start(s32[1,2,4]{2,1,0:T(2,128)} %param.13) | copy-start | bytes 100
  115.3 0.9 copy-start.2
  117.2 34.7 %collective-permute-start.1 = (bf16[2,1024,256]{1,2,0:T(8,128)(2,1)}, bf16[2,1024,256]{1,2,0:T(8,128)(2,1)}, u32[]{:S(2)}, u32[]{:S(2)}) collective-permute-start(bf16[2,1024,256]{1,2,0:T(8,128)(2,1)} %pad_maximum_fusion.3), channel_id=1, source_target_pairs={{8,0},{16,8},{24,16},{32,24},{40,32},{48,40},{56,48},{64,56},{72,6... | collective-permute-start | bytes 3145736 | tf_op jit(solution)/shard_map/ppermute | solution.py:24
  119.2 32.7 %collective-permute-start = (bf16[2,1024,256]{1,2,0:T(8,128)(2,1)}, bf16[2,1024,256]{1,2,0:T(8,128)(2,1)}, u32[]{:S(2)}, u32[]{:S(2)}) collective-permute-start(bf16[2,1024,256]{1,2,0:T(8,128)(2,1)} %pad_maximum_fusion.3), channel_id=1, source_target_pairs={{0,8},{8,16},{16,24},{24,32},{32,40},{40,48},{48,56},{56,64},{64,7... | collective-permute-start | bytes 3145736 | tf_op jit(solution)/shard_map/ppermute | solution.py:22
  150.5 1.5 copy-start.3
  150.5 1.5 copy-start.5
  154.3 1.6 copy-start.9
  154.3 1.6 copy-start.10
  154.4 1.6 copy-start.11
  155.9 12.8 %copy-start.7 = (bf16[2,1024,512]{1,2,0:T(8,128)(2,1)}, bf16[2,1024,512]{1,2,0:T(8,128)(2,1)S(1)}, u32[]{:S(2)}) copy-start(bf16[2,1024,512]{1,2,0:T(8,128)(2,1)S(1)} %get-tuple-element.39) | copy-start | bytes 6291460
  171.3 3.3 %copy-start.1 = (f32[3,1024,256]{1,2,0:T(8,128)S(1)}, f32[3,1024,256]{1,2,0:T(8,128)}, u32[]{:S(2)}) copy-start(f32[3,1024,256]{1,2,0:T(8,128)} %copy.27) | copy-start | bytes 9437188
